TPU v7x, 512 devices: a whole 4x8x8 slice. The times are simulated.
512 devices in a mesh: seq: 64 (over z, y), head: 8 (over x, core).
Axes of the slice: x: 4, y: 8, z: 8, core: 2. Of those that a mesh axis runs over, the one named last changes fastest.
Arguments:
- queries: bfloat16 [32768, 4096], P('seq', 'head'), may hold values from -6 to 6
- keys: bfloat16 [32768, 4096], P('seq', 'head'), may hold values from -6 to 6
- decay_log: float32 [32768, 4096], P('seq', 'head'), may hold values from -0.5 to 0, as said below
- write_rate: float32 [32, 32768], P('head', 'seq'), may hold values from 0 to 0.5, as said below
- output_grad: bfloat16 [32768, 4096], P(('seq', 'head')), may hold values from -15 to 15
Outputs:
- value_grad: bfloat16 [32768, 4096], P('seq', 'head')
Inputs may be any that keep to these rules, and one draw needn't show every extreme that they name: `decay_log`: every entry is negative or zero; which heads and channels decay fast varies with the seed and along the sequence. `write_rate`: every entry is positive; the strength varies with the seed over heads and along the sequence.
All inputs are finite; a program needn't handle non-finite values.
Results may differ from a plain program's by a relative error of at most 0.001.
Values may be sent and summed in bfloat16 or wider, within the bound.
No kernel may reach another device: no remote copies, remote signals or barrier semaphores. Data moves between devices by JAX's collectives and lax.ppermute only.
A program may use at most 128 MiB of HBM per device.

v0:
```python
import jax
import jax.numpy as jnp
from jax import lax
from jax.experimental import pallas as pl
from jax.experimental.pallas import tpu as pltpu
from jax.sharding import Mesh, PartitionSpec as P

HEAD_DIM = 128
CHUNK = 128
HALF = 64
ROWS = 8
PACKET = HEAD_DIM + HALF

epsilon = 1e-06
F32 = jnp.float32
BF16 = jnp.bfloat16


def split(values):
    high = values.astype(BF16)
    return high, (values - high.astype(F32)).astype(BF16)


def dot(left, right):
    return lax.dot_general(left, right, (((1,), (0,)), ((), ())), preferred_element_type=F32)


def product(left, right):
    left_high, left_low = left
    right_high, right_low = right
    both = jnp.concatenate([left_high, left_low], axis=1)
    return dot(both, jnp.concatenate([right_high, right_high], axis=0)) + dot(left_high, right_low)


def exact_right(left, right):
    left_high, left_low = left
    both = jnp.concatenate([left_high, left_low], axis=1)
    return dot(both, jnp.concatenate([right, right], axis=0))


def indices(size):
    shape = (size, size)
    return lax.broadcasted_iota(jnp.int32, shape, 0), lax.broadcasted_iota(jnp.int32, shape, 1)


def unit_upper_inverses(strict_parts, row, col):
    size = row.shape[0]

    def above(parts, step):
        keep = (row // (2 * step) == col // (2 * step)) & (row // step < col // step)
        return [jnp.where(keep, part, 0.0) for part in parts]

    eye = jnp.where(row == col, 1.0, 0.0)
    inverses = [eye - part for part in above(strict_parts, 1)]
    step = 2
    while step < size:
        blocks = [split(part) for part in above(strict_parts, step)]
        pairs = [split(inverse) for inverse in inverses]
        if step < 8:
            left = [product(pair, block) for pair, block in zip(pairs, blocks)]
            left = [product(split(part), pair) for part, pair in zip(left, pairs)]
            inverses = [inverse - part for inverse, part in zip(inverses, left)]
        else:
            starts = range(0, size, 2 * step)
            upper = [
                split(jnp.concatenate([inverse[s : s + step] for s in starts], axis=0))
                for inverse in inverses
            ]
            left = [product(pair, block) for pair, block in zip(upper, blocks)]
            left = [product(split(part), pair) for part, pair in zip(left, pairs)]
            merged = []
            for inverse, part in zip(inverses, left):
                pieces = []
                for place, s in enumerate(starts):
                    pieces.append(
                        inverse[s : s + step] - part[place * step : (place + 1) * step]
                    )
                    pieces.append(inverse[s + step : s + 2 * step])
                merged.append(jnp.concatenate(pieces, axis=0))
            inverses = merged
        step = step * 2
    return inverses


def as_column(line, row, col):
    return jnp.sum(jnp.where(row == col, line, 0.0), axis=1, keepdims=True)


def maps_kernel(
    queries_ref, keys_ref, decay_ref, rate_ref,
    trans_ref, lift_ref, carry_ref, reply_ref, step_ref, source_ref,
):
    row, col = indices(CHUNK)
    count = queries_ref.shape[0] // CHUNK
    chunks = [pl.ds(n * CHUNK, CHUNK) for n in range(count)]
    lower = jnp.where(row >= col, 1.0, 0.0).astype(BF16)
    lower_twice = jnp.concatenate([lower, lower], axis=1)

    sums = []
    for chunk in chunks:
        decay = decay_ref[chunk, :]
        high, rest = split(decay)
        rest_value = decay - high.astype(F32) - rest.astype(F32)
        sums.append(
            dot(lower_twice, jnp.concatenate([high, rest], axis=0))
            + dot(lower, rest_value.astype(BF16))
        )
    ends = [jnp.exp(total[CHUNK - 1 :, :]) for total in sums]
    behind, ahead, carry = [], [], []
    for n, chunk in enumerate(chunks):
        keys = keys_ref[chunk, :].astype(F32)
        queries = queries_ref[chunk, :].astype(F32)
        keys_scale = lax.rsqrt(jnp.sum(keys * keys, axis=1, keepdims=True) + epsilon)
        queries_scale = lax.rsqrt(jnp.sum(queries * queries, axis=1, keepdims=True) + epsilon)
        rate = as_column(rate_ref[0, :, chunk], row, col)
        grown = jnp.exp(-sums[n])
        shrunk = jnp.exp(sums[n])
        keys = keys * keys_scale
        keys_behind = keys * grown
        behind.append(split(keys_behind))
        carry.append(keys_behind * ends[n])
        stacked = jnp.concatenate([keys * (shrunk * rate), queries * (shrunk * queries_scale)], axis=0)
        ahead.append(stacked.T)
    ahead_pairs = [split(part) for part in ahead]
    scores = [product(left, right) for left, right in zip(behind, ahead_pairs)]
    strict = [jnp.where(col > row, part[:, :CHUNK], 0.0) for part in scores]
    inverses = unit_upper_inverses(strict, row, col)
    solved = []
    for n in range(count):
        queries_side = jnp.where(col >= row, scores[n][:, CHUNK:], 0.0)
        right = split(jnp.concatenate([queries_side, carry[n]], axis=1))
        solved.append(product(split(inverses[n]), right))
    source, trans = [], []
    for n, chunk in enumerate(chunks):
        high, low = ahead_pairs[n]
        taken = product((high[:, :CHUNK], low[:, :CHUNK]), split(solved[n]))
        source.append(ahead[n][:, CHUNK:] - taken[:, :HEAD_DIM])
        trans.append(jnp.where(row == col, ends[n], 0.0) - taken[:, HEAD_DIM:])
        reply_ref[0, chunk, :] = solved[n][:, :CHUNK]
        carry_ref[0, chunk, :] = solved[n][:, CHUNK:]
        source_ref[0, chunk, :] = source[n]
        step_ref[0, chunk, :] = trans[n]
    parts = [(trans[n], [source[n]]) for n in range(count)]
    while len(parts) > 1:
        merged = []
        for n in range(0, len(parts), 2):
            first, later = parts[n], parts[n + 1]
            right = jnp.concatenate([later[0]] + later[1], axis=1)
            moved = product(split(first[0]), split(right))
            pieces = [moved[:, s : s + CHUNK] for s in range(HEAD_DIM, moved.shape[1], CHUNK)]
            merged.append((moved[:, :HEAD_DIM], first[1] + pieces))
        parts = merged
    trans_ref[0] = parts[0][0].T
    for n, part in enumerate(parts[0][1]):
        lift_ref[0, :, n * CHUNK : (n + 1) * CHUNK] = part


def packet_kernel(trans_ref, lift_ref, grads_ref, packet_ref):
    source = exact_right(split(lift_ref[0]), grads_ref[...]).T
    for place in range(2):
        packet_ref[place, :HEAD_DIM, :] = trans_ref[0]
        packet_ref[place, HEAD_DIM:, :] = source[place * HALF : (place + 1) * HALF]


def answer_kernel(
    carry_ref, reply_ref, step_ref, source_ref, rate_ref, grads_ref, gain_ref, own_ref
):
    row, col = indices(CHUNK)
    count = carry_ref.shape[1] // CHUNK
    chunks = [slice(n * CHUNK, (n + 1) * CHUNK) for n in range(count)]
    local = []
    for chunk in chunks:
        left = jnp.concatenate([reply_ref[0, chunk, :], source_ref[0, chunk, :]], axis=0)
        local.append(exact_right(split(left), grads_ref[chunk, :]))
    behind = None
    for n in reversed(range(count)):
        chunk = chunks[n]
        rate = as_column(rate_ref[0, :, chunk], row, col)
        own = local[n][:CHUNK]
        gain = carry_ref[0, chunk, :]
        if behind is not None:
            moved = product(split(gain), behind)
            gain = moved[:, :HEAD_DIM]
            own = own + moved[:, HEAD_DIM:]
        high, low = split(gain * rate)
        gain_ref[0, chunk, :HEAD_DIM] = high
        gain_ref[0, chunk, HEAD_DIM:] = low
        own_ref[0, chunk, :] = own * rate
        if n:
            trans = step_ref[0, chunk, :]
            source = local[n][CHUNK:]
            if behind is not None:
                moved = product(split(trans), behind)
                trans = moved[:, :HEAD_DIM]
                source = source + moved[:, HEAD_DIM:]
            behind = split(jnp.concatenate([trans, source], axis=1))


def with_source(moved, source):
    return jnp.concatenate([moved[:HEAD_DIM], moved[HEAD_DIM:] + source], axis=0)


def joined(first, later):
    moved = product(split(later), split(first[:HEAD_DIM]))
    return with_source(moved, first[HEAD_DIM:])


def row_kernel(maps_ref, total_ref, some_ref):
    maps = [maps_ref[n] for n in range(ROWS)]
    pairs = [joined(maps[n], maps[n + 1]) for n in range(0, ROWS, 2)]
    fours = [joined(pairs[0], pairs[1]), joined(pairs[2], pairs[3])]
    total = joined(fours[0], fours[1])
    for n in range(ROWS):
        total_ref[n] = total
    some_ref[0] = pairs[1]
    some_ref[1] = pairs[3]
    some_ref[2] = fours[1]


def suffix_kernel(maps_ref, some_ref, suffix_ref):
    pair_second, pair_last, four_last = some_ref[0], some_ref[1], some_ref[2]
    suffix_ref[6] = maps_ref[7]
    suffix_ref[5] = pair_last
    suffix_ref[4] = joined(maps_ref[5], pair_last)
    suffix_ref[3] = four_last
    suffix_ref[2] = joined(maps_ref[3], four_last)
    from_second = joined(pair_second, four_last)
    suffix_ref[1] = from_second
    suffix_ref[0] = joined(maps_ref[1], from_second)


def state_kernel(place_ref, totals_ref, suffix_ref, states_ref):
    place = place_ref[0]
    row = lax.broadcasted_iota(jnp.int32, (PACKET, HEAD_DIM), 0)
    col = lax.broadcasted_iota(jnp.int32, (PACKET, HEAD_DIM), 1)
    identity = jnp.where(row == col, 1.0, 0.0)
    maps = [jnp.where(n > place, totals_ref[n], identity) for n in range(ROWS)]
    pairs = [joined(maps[n], maps[n + 1]) for n in (2, 4, 6)]
    front = joined(maps[1], pairs[0])
    back = joined(pairs[1], pairs[2])
    state = product(split(back[HEAD_DIM:]), split(front[:HEAD_DIM])) + front[HEAD_DIM:]
    states_ref[ROWS - 1] = state
    state = split(state)
    for n in range(ROWS - 1):
        moved = product(state, split(suffix_ref[n, :HEAD_DIM, :]))
        states_ref[n] = moved + suffix_ref[n, HEAD_DIM:, :]


def result_kernel(gain_ref, own_ref, state_ref, out_ref):
    high, low = split(state_ref[0])

    def against(left, right):
        return lax.dot_general(
            left, right, (((1,), (1,)), ((), ())), preferred_element_type=F32
        )

    moved = against(gain_ref[0], jnp.concatenate([high, high], axis=1))
    moved = moved + against(gain_ref[0, :, :HEAD_DIM], low)
    out_ref[...] = (own_ref[0] + moved).astype(BF16)


def per_head(*shape):
    return pl.BlockSpec((1,) + shape, lambda h: (h,) + (0,) * len(shape))


def params():
    return pltpu.CompilerParams(vmem_limit_bytes=48 * 1024 * 1024)


def whole(kernel, out_shapes, *args, scalar=False):
    vmem = pl.BlockSpec(memory_space=pltpu.VMEM)
    specs = [vmem] * len(args)
    if scalar:
        specs[0] = pl.BlockSpec(memory_space=pltpu.SMEM)
    return pl.pallas_call(
        kernel,
        out_shape=[jax.ShapeDtypeStruct(shape, F32) for shape in out_shapes],
        in_specs=specs,
        out_specs=[vmem] * len(out_shapes),
        compiler_params=params(),
    )(*args)


def local(queries, keys, decay_log, write_rate, output_grad):
    heads, tokens = write_rate.shape
    gathered = lax.all_to_all(output_grad, "head", split_axis=1, concat_axis=0, tiled=True)
    rates = write_rate.reshape(heads, 1, tokens)
    lanes = pl.BlockSpec((tokens, HEAD_DIM), lambda h: (0, h))
    square = per_head(HEAD_DIM, HEAD_DIM)
    tall = per_head(tokens, HEAD_DIM)

    def shape(*dims, dtype=F32):
        return jax.ShapeDtypeStruct((heads,) + dims, dtype)

    trans, lift, carry, reply, steps, sources = pl.pallas_call(
        maps_kernel,
        grid=(heads,),
        in_specs=[lanes, lanes, lanes, per_head(1, tokens)],
        out_specs=[square, per_head(HEAD_DIM, tokens), tall, tall, tall, tall],
        out_shape=[
            shape(HEAD_DIM, HEAD_DIM), shape(HEAD_DIM, tokens),
            shape(tokens, HEAD_DIM), shape(tokens, HEAD_DIM),
            shape(tokens, HEAD_DIM), shape(tokens, HEAD_DIM),
        ],
        compiler_params=params(),
    )(queries, keys, decay_log, rates)
    packet = pl.pallas_call(
        packet_kernel,
        grid=(heads,),
        in_specs=[square, per_head(HEAD_DIM, tokens), lanes],
        out_specs=pl.BlockSpec((2, PACKET, HEAD_DIM), lambda h: (h, 0, 0)),
        out_shape=jax.ShapeDtypeStruct((2 * heads, PACKET, HEAD_DIM), F32),
        compiler_params=params(),
    )(trans, lift, gathered)
    maps = lax.all_to_all(packet, "y", 0, 0, tiled=True)
    gain, own = pl.pallas_call(
        answer_kernel,
        grid=(heads,),
        in_specs=[tall, tall, tall, tall, per_head(1, tokens), lanes],
        out_specs=[per_head(tokens, 2 * HEAD_DIM), tall],
        out_shape=[shape(tokens, 2 * HEAD_DIM, dtype=BF16), shape(tokens, HEAD_DIM)],
        compiler_params=params(),
    )(carry, reply, steps, sources, rates, gathered)
    total, some = whole(row_kernel, [(ROWS, PACKET, HEAD_DIM), (3, PACKET, HEAD_DIM)], maps)
    totals = lax.all_to_all(total, "z", 0, 0, tiled=True)
    (suffix,) = whole(suffix_kernel, [(ROWS - 1, PACKET, HEAD_DIM)], maps, some)
    place = lax.axis_index("z").astype(jnp.int32).reshape(1)
    (states,) = whole(
        state_kernel, [(ROWS, HALF, HEAD_DIM)], place, totals, suffix, scalar=True
    )
    states = lax.all_to_all(states, "y", 0, 0, tiled=True).reshape(heads, HEAD_DIM, HEAD_DIM)
    return pl.pallas_call(
        result_kernel,
        grid=(heads,),
        in_specs=[per_head(tokens, 2 * HEAD_DIM), tall, square],
        out_specs=lanes,
        out_shape=jax.ShapeDtypeStruct((tokens, heads * HEAD_DIM), BF16),
        compiler_params=params(),
    )(gain, own, states)


def solution(mesh):
    seq, head = mesh.devices.shape
    grid = Mesh(mesh.devices.reshape(seq // ROWS, ROWS, head), ("z", "y", "head"))
    tokens = ("z", "y")
    return jax.shard_map(
        local,
        mesh=grid,
        in_specs=(
            P(tokens, "head"),
            P(tokens, "head"),
            P(tokens, "head"),
            P("head", tokens),
            P(("z", "y", "head"), None),
        ),
        out_specs=P(tokens, "head"),
        check_vma=False,
    )
```

profile of v0, /device:TPU:1, one launch (start us, length us, event | category | flops | bytes accessed | tf_op | source)
XLA Modules:
  0.0 110.9 jit_solution(14066518452723043106)
XLA Ops:
  0.0 0.0 copy-start.8
  0.0 1.9 %copy.9 = bf16[8,8,8,512]{3,2,0,1:T(8,128)(2,1)} copy(bf16[8,8,8,512]{3,2,1,0:T(8,128)(2,1)} %bitcast.12) | data formatting | bytes 1048576 | tf_op jit(solution)/shard_map/all_to_all | solution.py:286
  1.9 0.0 copy-start.6
  1.9 0.0 copy-start.7
  1.9 10.4 %all-to-all-start = ((bf16[64,8,512]{2,0,1:T(8,128)(2,1)}), bf16[64,8,512]{2,0,1:T(8,128)(2,1)S(1)}, u32[]{:S(2)}, u32[]{:S(2)}) async-start(bf16[64,8,512]{2,0,1:T(8,128)(2,1)} %bitcast.8), calls=%async_computation | async-start | bytes 1048576 | tf_op jit(solution)/shard_map/all_to_all | solution.py:286
  12.3 0.0 copy-done.8
  12.3 0.0 copy-done.6
  12.3 0.0 copy-done.7
  12.3 14.3 %shard_map.55 = (f32[4,128,128]{2,1,0:T(8,128)S(1)}, f32[4,128,512]{2,1,0:T(8,128)S(1)}, f32[4,512,128]{2,1,0:T(8,128)S(1)}, f32[4,512,128]{2,1,0:T(8,128)S(1)},...) custom-call(bf16[512,512]{1,0:T(8,128)(2,1)S(1)} %copy-done.6, bf16[512,512]{1,0:T(8,128)(2,1)S(1)} %copy-done.7, ...), custom_call_target="tpu_custom_call" | custom-call | tf_op jit(solution)/shard_map/pallas_call | solution.py:295
  26.6 0.0 copy-start
  26.6 1.0 copy-done
  27.6 0.0 copy-start.2
  27.6 1.0 copy-done.2
  28.6 0.0 copy-start.4
  28.6 1.0 copy-done.4
  29.6 0.0 all-to-all-done
  29.6 1.3 %shard_map.57 = f32[8,192,128]{2,1,0:T(8,128)S(1)} custom-call(f32[4,128,128]{2,1,0:T(8,128)S(1)} %get-tuple-element.21.trans_ref, f32[4,128,512]{2,1,0:T(8,128)S(1)} %get-tuple-element.22.lift_ref, bf16[512,512]{1,0:T(8,128)(2,1)S(1)} %bitcast.9), custom_call_target="tpu_custom_call" | custom-call | tf_op jit(solution)/shard_map/pallas_call | solution.py:307
  30.9 26.0 %all_to_all.34.maps_ref = f32[8,192,128]{2,1,0:T(8,128)S(1)} all-to-all(f32[8,192,128]{2,1,0:T(8,128)S(1)} %shard_map.57), channel_id=1, replica_groups=mesh['z'=8,'y'=8,'head'=8] {'y'}, dimensions={0} | all-to-all | bytes 1572864 | tf_op jit(solution)/shard_map/all_to_all | solution.py:315
  56.9 1.5 %shard_map.58 = (f32[8,192,128]{2,1,0:T(8,128)}, f32[3,192,128]{2,1,0:T(8,128)S(1)}) custom-call(f32[8,192,128]{2,1,0:T(8,128)S(1)} %all_to_all.34.maps_ref), custom_call_target="tpu_custom_call" | custom-call | tf_op jit(solution)/shard_map/pallas_call | solution.py:275
  58.4 9.8 %all-to-all-start.2 = ((f32[8,192,128]{2,1,0:T(8,128)}), f32[8,192,128]{2,1,0:T(8,128)S(1)}, u32[]{:S(2)}, u32[]{:S(2)}) async-start(f32[8,192,128]{2,1,0:T(8,128)} %get-tuple-element.23), calls=%async_computation.2 | async-start | bytes 1572864 | tf_op jit(solution)/shard_map/all_to_all | solution.py:325
  68.2 0.5 shard_map.59.suffix_ref
  68.7 23.1 %all-to-all-done.2.totals_ref = f32[8,192,128]{2,1,0:T(8,128)S(1)} async-done(((f32[8,192,128]{2,1,0:T(8,128)}), f32[8,192,128]{2,1,0:T(8,128)S(1)}, u32[]{:S(2)}, u32[]{:S(2)}) %all-to-all-start.2) | async-done | bytes 786464 | tf_op jit(solution)/shard_map/all_to_all | solution.py:325
  91.8 1.5 %shard_map.60 = f32[8,64,128]{2,1,0:T(8,128)} custom-call(s32[1]{0:T(128)} %bitcast.2.place_ref, f32[8,192,128]{2,1,0:T(8,128)S(1)} %all-to-all-done.2.totals_ref, f32[7,192,128]{2,1,0:T(8,128)S(1)} %shard_map.59.suffix_ref), custom_call_target="tpu_custom_call" | custom-call | tf_op jit(solution)/shard_map/pallas_call | solution.py:275
  93.3 3.4 %all-to-all-start.3 = ((f32[8,64,128]{2,1,0:T(8,128)}), f32[8,64,128]{2,1,0:T(8,128)S(1)}, u32[]{:S(2)}, u32[]{:S(2)}) async-start(f32[8,64,128]{2,1,0:T(8,128)} %shard_map.60), calls=%async_computation.3 | async-start | bytes 524288 | tf_op jit(solution)/shard_map/all_to_all | solution.py:331
  96.7 0.0 copy-start.1
  96.7 1.2 %copy-done.1 = f32[4,512,128]{2,1,0:T(8,128)S(1)} copy-done((f32[4,512,128]{2,1,0:T(8,128)S(1)}, f32[4,512,128]{2,1,0:T(8,128)}, u32[]{:S(2)}) %copy-start.1) | copy-done | bytes 1048600
  97.9 0.0 copy-start.3
  97.9 1.2 %copy-done.3 = f32[4,512,128]{2,1,0:T(8,128)S(1)} copy-done((f32[4,512,128]{2,1,0:T(8,128)S(1)}, f32[4,512,128]{2,1,0:T(8,128)}, u32[]{:S(2)}) %copy-start.3) | copy-done | bytes 1048600
  99.1 0.0 copy-start.5
  99.1 1.2 %copy-done.5 = f32[4,512,128]{2,1,0:T(8,128)S(1)} copy-done((f32[4,512,128]{2,1,0:T(8,128)S(1)}, f32[4,512,128]{2,1,0:T(8,128)}, u32[]{:S(2)}) %copy-start.5) | copy-done | bytes 1048600
  100.4 4.7 %shard_map.56 = (bf16[4,512,256]{2,1,0:T(8,128)(2,1)S(1)}, f32[4,512,128]{2,1,0:T(8,128)S(1)}) custom-call(f32[4,512,128]{2,1,0:T(8,128)S(1)} %copy-done.1, f32[4,512,128]{2,1,0:T(8,128)S(1)} %copy-done.3, f32[4,512,128]{2,1,0:T(8,128)S(1)} %copy-done.5, f32[4,512,128]{2,1,0:T(8,128)} %get-tuple-element.18.source_ref, f32[4,1,512]{2,1,0:T(1,128)S(1)} %reshape.12.rate_ref, ...), custom_call_target="tpu_custom_call" | custom-call | tf_op jit(solution)/shard_map/pallas_call | solution.py:316
  105.1 3.7 %all-to-all-done.3 = f32[8,64,128]{2,1,0:T(8,128)S(1)} async-done(((f32[8,64,128]{2,1,0:T(8,128)}), f32[8,64,128]{2,1,0:T(8,128)S(1)}, u32[]{:S(2)}, u32[]{:S(2)}) %all-to-all-start.3) | async-done | bytes 262176 | tf_op jit(solution)/shard_map/all_to_all | solution.py:331
  108.8 2.1 %shard_map.61 = bf16[512,512]{1,0:T(8,128)(2,1)} custom-call(bf16[4,512,256]{2,1,0:T(8,128)(2,1)S(1)} %get-tuple-element.19.gain_ref, f32[4,512,128]{2,1,0:T(8,128)S(1)} %get-tuple-element.20.own_ref, f32[4,128,128]{2,1,0:T(8,128)S(1)} %bitcast.11), custom_call_target="tpu_custom_call" | custom-call | tf_op jit(solution)/shard_map/pallas_call | solution.py:332
  (1 shorter events, 0.0 us)
Async XLA Ops:
  0.0 12.3 %copy-start.8 = (f32[4,512]{1,0:T(4,128)S(1)}, f32[4,512]{1,0:T(4,128)}, u32[]{:S(2)}) copy-start(f32[4,512]{1,0:T(4,128)} %param.8) | copy-start | bytes 24580
  1.9 10.4 %copy-start.6 = (bf16[512,512]{1,0:T(8,128)(2,1)S(1)}, bf16[512,512]{1,0:T(8,128)(2,1)}, u32[]{:S(2)}) copy-start(bf16[512,512]{1,0:T(8,128)(2,1)} %queries_ref.1) | copy-start | bytes 1572868
  1.9 10.4 %copy-start.7 = (bf16[512,512]{1,0:T(8,128)(2,1)S(1)}, bf16[512,512]{1,0:T(8,128)(2,1)}, u32[]{:S(2)}) copy-start(bf16[512,512]{1,0:T(8,128)(2,1)} %keys_ref.1) | copy-start | bytes 1572868
  1.9 27.7 %all-to-all-start = ((bf16[64,8,512]{2,0,1:T(8,128)(2,1)}), bf16[64,8,512]{2,0,1:T(8,128)(2,1)S(1)}, u32[]{:S(2)}, u32[]{:S(2)}) async-start(bf16[64,8,512]{2,0,1:T(8,128)(2,1)} %bitcast.8), calls=%async_computation | async-start | bytes 1048576 | tf_op jit(solution)/shard_map/all_to_all | solution.py:286
  26.6 1.0 copy-start
  27.6 1.0 copy-start.2
  28.6 1.0 copy-start.4
  58.4 33.3 %all-to-all-start.2 = ((f32[8,192,128]{2,1,0:T(8,128)}), f32[8,192,128]{2,1,0:T(8,128)S(1)}, u32[]{:S(2)}, u32[]{:S(2)}) async-start(f32[8,192,128]{2,1,0:T(8,128)} %get-tuple-element.23), calls=%async_computation.2 | async-start | bytes 1572864 | tf_op jit(solution)/shard_map/all_to_all | solution.py:325
  93.3 15.5 %all-to-all-start.3 = ((f32[8,64,128]{2,1,0:T(8,128)}), f32[8,64,128]{2,1,0:T(8,128)S(1)}, u32[]{:S(2)}, u32[]{:S(2)}) async-start(f32[8,64,128]{2,1,0:T(8,128)} %shard_map.60), calls=%async_computation.3 | async-start | bytes 524288 | tf_op jit(solution)/shard_map/all_to_all | solution.py:331
  96.7 1.2 %copy-start.1 = (f32[4,512,128]{2,1,0:T(8,128)S(1)}, f32[4,512,128]{2,1,0:T(8,128)}, u32[]{:S(2)}) copy-start(f32[4,512,128]{2,1,0:T(8,128)} %copy-done) | copy-start | bytes 3145732
  97.9 1.2 %copy-start.3 = (f32[4,512,128]{2,1,0:T(8,128)S(1)}, f32[4,512,128]{2,1,0:T(8,128)}, u32[]{:S(2)}) copy-start(f32[4,512,128]{2,1,0:T(8,128)} %copy-done.2) | copy-start | bytes 3145732
  99.1 1.2 %copy-start.5 = (f32[4,512,128]{2,1,0:T(8,128)S(1)}, f32[4,512,128]{2,1,0:T(8,128)}, u32[]{:S(2)}) copy-start(f32[4,512,128]{2,1,0:T(8,128)} %copy-done.4) | copy-start | bytes 3145732
where the time goes:
time: 111 us
  waiting for transfers between devices  26.8 us (24%)
  blocking collectives  26 us (23%)
  Pallas kernels  25.9 us (23%)
  starting transfers between devices  23.6 us (21%)
  local copies, waits for them, and re-layouts  8.55 us (8%)
    all_to_all x1, blocking collectives, local(): maps = lax.all_to_all(packet, 'y', 0, 0, tiled=True)  26 us
    all_to_all x1, waiting for transfers between devices, local(): totals = lax.all_to_all(total, 'z', 0, 0, tiled=True)  23.1 us
    pallas_call x1, Pallas kernels, local(): pl.pallas_call(maps_kernel, grid=(heads,), in_specs=[lanes, lanes, lanes,...  14.3 us
    all_to_all x1, starting transfers between devices, local(): lax.all_to_all(output_grad, 'head', split_axis=1, concat_axis=0, tiled=True)  10.4 us
    all_to_all x1, starting transfers between devices, local(): totals = lax.all_to_all(total, 'z', 0, 0, tiled=True)  9.76 us
    unnamed x18, local copies, waits for them, and re-layouts  6.65 us
    pallas_call x1, Pallas kernels, local(): pl.pallas_call(answer_kernel, grid=(heads,), in_specs=[tall, tall, tall,...  4.72 us
    all_to_all x1, waiting for transfers between devices, local(): lax.all_to_all(states, 'y', 0, 0, tiled=True)  3.67 us
  transfers between devices with their start and end apart: 3, of which 2 were waited for; matrix products, arithmetic and copies ran while one was open for 0% of the time, Pallas kernels for 18%

commit v1 on v0

--- a/solution.py
+++ b/solution.py
@@ -10,6 +10,9 @@
 HALF = 64
 ROWS = 8
 PACKET = HEAD_DIM + HALF
+NOTES = 16
+LEVELS = 31990.0
+LOG_2 = 0.6931471805599453
 
 epsilon = 1e-06
 F32 = jnp.float32
@@ -29,7 +32,14 @@
     left_high, left_low = left
     right_high, right_low = right
     both = jnp.concatenate([left_high, left_low], axis=1)
-    return dot(both, jnp.concatenate([right_high, right_high], axis=0)) + dot(left_high, right_low)
+    width = right_high.shape[1]
+    if width > HEAD_DIM:
+        stacked = jnp.concatenate([right_high, right_high], axis=0)
+        return dot(both, stacked) + dot(left_high, right_low)
+    upper = jnp.concatenate([right_high, right_low], axis=1)
+    lower = jnp.concatenate([right_high, jnp.zeros_like(right_low)], axis=1)
+    parts = dot(both, jnp.concatenate([upper, lower], axis=0))
+    return parts[:, :width] + parts[:, width:]
 
 
 def exact_right(left, right):
@@ -88,17 +98,23 @@
 
 def maps_kernel(
     queries_ref, keys_ref, decay_ref, rate_ref,
-    trans_ref, lift_ref, carry_ref, reply_ref, step_ref, source_ref,
+    trans_ref, lift_ref, carry_out, reply_out, step_out, source_out,
+    carry_ref, reply_ref, step_ref, source_ref, sems,
 ):
     row, col = indices(CHUNK)
     count = queries_ref.shape[0] // CHUNK
-    chunks = [pl.ds(n * CHUNK, CHUNK) for n in range(count)]
+    heads = queries_ref.shape[1] // HEAD_DIM
+    places = [
+        (h, slice(n * CHUNK, (n + 1) * CHUNK), slice(h * HEAD_DIM, (h + 1) * HEAD_DIM))
+        for h in range(heads)
+        for n in range(count)
+    ]
     lower = jnp.where(row >= col, 1.0, 0.0).astype(BF16)
     lower_twice = jnp.concatenate([lower, lower], axis=1)
 
     sums = []
-    for chunk in chunks:
-        decay = decay_ref[chunk, :]
+    for _, chunk, lanes in places:
+        decay = decay_ref[chunk, lanes]
         high, rest = split(decay)
         rest_value = decay - high.astype(F32) - rest.astype(F32)
         sums.append(
@@ -107,12 +123,12 @@
         )
     ends = [jnp.exp(total[CHUNK - 1 :, :]) for total in sums]
     behind, ahead, carry = [], [], []
-    for n, chunk in enumerate(chunks):
-        keys = keys_ref[chunk, :].astype(F32)
-        queries = queries_ref[chunk, :].astype(F32)
+    for n, (h, chunk, lanes) in enumerate(places):
+        keys = keys_ref[chunk, lanes].astype(F32)
+        queries = queries_ref[chunk, lanes].astype(F32)
         keys_scale = lax.rsqrt(jnp.sum(keys * keys, axis=1, keepdims=True) + epsilon)
         queries_scale = lax.rsqrt(jnp.sum(queries * queries, axis=1, keepdims=True) + epsilon)
-        rate = as_column(rate_ref[0, :, chunk], row, col)
+        rate = as_column(rate_ref[h, :, chunk], row, col)
         grown = jnp.exp(-sums[n])
         shrunk = jnp.exp(sums[n])
         keys = keys * keys_scale
@@ -126,22 +142,34 @@
     strict = [jnp.where(col > row, part[:, :CHUNK], 0.0) for part in scores]
     inverses = unit_upper_inverses(strict, row, col)
     solved = []
-    for n in range(count):
+    for n in range(len(places)):
         queries_side = jnp.where(col >= row, scores[n][:, CHUNK:], 0.0)
         right = split(jnp.concatenate([queries_side, carry[n]], axis=1))
         solved.append(product(split(inverses[n]), right))
+        h, chunk, _ = places[n]
+        reply_ref[h, chunk, :] = solved[n][:, :CHUNK]
+        carry_ref[h, chunk, :] = solved[n][:, CHUNK:]
+    copies = [
+        pltpu.make_async_copy(kept, late, sems.at[n])
+        for n, (kept, late) in enumerate(
+            [(carry_ref, carry_out), (reply_ref, reply_out),
+             (step_ref, step_out), (source_ref, source_out)]
+        )
+    ]
+    for copy in copies[:2]:
+        copy.start()
     source, trans = [], []
-    for n, chunk in enumerate(chunks):
+    for n, (h, chunk, _) in enumerate(places):
         high, low = ahead_pairs[n]
         taken = product((high[:, :CHUNK], low[:, :CHUNK]), split(solved[n]))
         source.append(ahead[n][:, CHUNK:] - taken[:, :HEAD_DIM])
         trans.append(jnp.where(row == col, ends[n], 0.0) - taken[:, HEAD_DIM:])
-        reply_ref[0, chunk, :] = solved[n][:, :CHUNK]
-        carry_ref[0, chunk, :] = solved[n][:, CHUNK:]
-        source_ref[0, chunk, :] = source[n]
-        step_ref[0, chunk, :] = trans[n]
-    parts = [(trans[n], [source[n]]) for n in range(count)]
-    while len(parts) > 1:
+        source_ref[h, chunk, :] = source[n]
+        step_ref[h, chunk, :] = trans[n]
+    for copy in copies[2:]:
+        copy.start()
+    parts = [(trans[n], [source[n]]) for n in range(len(places))]
+    while len(parts) > heads:
         merged = []
         for n in range(0, len(parts), 2):
             first, later = parts[n], parts[n + 1]
@@ -150,16 +178,76 @@
             pieces = [moved[:, s : s + CHUNK] for s in range(HEAD_DIM, moved.shape[1], CHUNK)]
             merged.append((moved[:, :HEAD_DIM], first[1] + pieces))
         parts = merged
-    trans_ref[0] = parts[0][0].T
-    for n, part in enumerate(parts[0][1]):
-        lift_ref[0, :, n * CHUNK : (n + 1) * CHUNK] = part
+    for h, (turned, pieces) in enumerate(parts):
+        trans_ref[h] = turned.T
+        for n, part in enumerate(pieces):
+            lift_ref[h, :, n * CHUNK : (n + 1) * CHUNK] = part
+    for copy in copies:
+        copy.wait()
+
+
+def power_of_two(exponent):
+    return jnp.exp(exponent * LOG_2)
+
+
+def coded(values):
+    scale = jnp.max(jnp.abs(values), axis=0, keepdims=True) * 1.01
+    scale = jnp.maximum(scale.astype(BF16).astype(F32), 1e-30)
+    steps = jnp.floor(jnp.abs(values) * (LEVELS / scale) + 0.5)
+    exponent = jnp.floor(steps * (1.0 / 128.0))
+    fraction = steps - exponent * 128.0
+    carrier = (1.0 + fraction * (1.0 / 128.0)) * power_of_two(exponent - 125.0)
+    return jnp.where(values < 0.0, -carrier, carrier).astype(BF16), scale
+
+
+def decoded(carrier, scale):
+    carrier = carrier.astype(F32)
+    size = jnp.abs(carrier)
+    exponent = jnp.floor(jnp.log(size * (1.0 + 1.0 / 512.0)) * (1.0 / LOG_2))
+    fraction = jnp.floor((size * power_of_two(-exponent) - 1.0) * 128.0 + 0.5)
+    steps = (exponent + 125.0) * 128.0 + fraction
+    return jnp.where(carrier < 0.0, -steps, steps) * (scale * (1.0 / LEVELS))
+
+
+def notes_of(*lines):
+    pad = jnp.zeros((NOTES - len(lines), HEAD_DIM), F32)
+    return jnp.concatenate(list(lines) + [pad], axis=0).astype(BF16)
+
+
+def coded_trans(trans):
+    row, col = indices(HEAD_DIM)
+    diagonal = jnp.sum(jnp.where(row == col, trans, 0.0), axis=0, keepdims=True)
+    carrier, scale = coded(jnp.where(row == col, 0.0, trans))
+    high, middle = split(diagonal)
+    high, middle = high.astype(F32), middle.astype(F32)
+    return carrier, (scale, high, middle, diagonal - high - middle)
+
+
+def decoded_map(ref, place):
+    row, col = indices(HEAD_DIM)
+    notes = ref[place, PACKET:, :].astype(F32)
+    diagonal = notes[2:3] + notes[3:4] + notes[4:5]
+    trans = decoded(ref[place, :HEAD_DIM, :], notes[0:1])
+    source = decoded(ref[place, HEAD_DIM:PACKET, :], notes[1:2])
+    return jnp.concatenate([jnp.where(row == col, diagonal, trans), source], axis=0)
+
+
+def pieces_kernel(grads_ref, pieces_ref):
+    count, _, width = pieces_ref.shape
+    for n in range(count):
+        pieces_ref[n] = grads_ref[:, n * width : (n + 1) * width]
 
 
 def packet_kernel(trans_ref, lift_ref, grads_ref, packet_ref):
-    source = exact_right(split(lift_ref[0]), grads_ref[...]).T
-    for place in range(2):
-        packet_ref[place, :HEAD_DIM, :] = trans_ref[0]
-        packet_ref[place, HEAD_DIM:, :] = source[place * HALF : (place + 1) * HALF]
+    for h in range(trans_ref.shape[0]):
+        grads = grads_ref[:, h * HEAD_DIM : (h + 1) * HEAD_DIM]
+        source = exact_right(split(lift_ref[h]), grads).T
+        trans, lines = coded_trans(trans_ref[h])
+        for place in range(2):
+            half, scale = coded(source[place * HALF : (place + 1) * HALF])
+            packet_ref[2 * h + place, :HEAD_DIM, :] = trans
+            packet_ref[2 * h + place, HEAD_DIM:PACKET, :] = half
+            packet_ref[2 * h + place, PACKET:, :] = notes_of(lines[0], scale, *lines[1:])
 
 
 def answer_kernel(
@@ -206,12 +294,17 @@
 
 
 def row_kernel(maps_ref, total_ref, some_ref):
-    maps = [maps_ref[n] for n in range(ROWS)]
+    maps = [decoded_map(maps_ref, n) for n in range(ROWS)]
     pairs = [joined(maps[n], maps[n + 1]) for n in range(0, ROWS, 2)]
     fours = [joined(pairs[0], pairs[1]), joined(pairs[2], pairs[3])]
     total = joined(fours[0], fours[1])
+    trans, lines = coded_trans(total[:HEAD_DIM])
+    source, scale = coded(total[HEAD_DIM:])
+    notes = notes_of(lines[0], scale, *lines[1:])
     for n in range(ROWS):
-        total_ref[n] = total
+        total_ref[n, :HEAD_DIM, :] = trans
+        total_ref[n, HEAD_DIM:PACKET, :] = source
+        total_ref[n, PACKET:, :] = notes
     some_ref[0] = pairs[1]
     some_ref[1] = pairs[3]
     some_ref[2] = fours[1]
@@ -219,14 +312,14 @@
 
 def suffix_kernel(maps_ref, some_ref, suffix_ref):
     pair_second, pair_last, four_last = some_ref[0], some_ref[1], some_ref[2]
-    suffix_ref[6] = maps_ref[7]
+    suffix_ref[6] = decoded_map(maps_ref, 7)
     suffix_ref[5] = pair_last
-    suffix_ref[4] = joined(maps_ref[5], pair_last)
+    suffix_ref[4] = joined(decoded_map(maps_ref, 5), pair_last)
     suffix_ref[3] = four_last
-    suffix_ref[2] = joined(maps_ref[3], four_last)
+    suffix_ref[2] = joined(decoded_map(maps_ref, 3), four_last)
     from_second = joined(pair_second, four_last)
     suffix_ref[1] = from_second
-    suffix_ref[0] = joined(maps_ref[1], from_second)
+    suffix_ref[0] = joined(decoded_map(maps_ref, 1), from_second)
 
 
 def state_kernel(place_ref, totals_ref, suffix_ref, states_ref):
@@ -234,109 +327,134 @@
     row = lax.broadcasted_iota(jnp.int32, (PACKET, HEAD_DIM), 0)
     col = lax.broadcasted_iota(jnp.int32, (PACKET, HEAD_DIM), 1)
     identity = jnp.where(row == col, 1.0, 0.0)
-    maps = [jnp.where(n > place, totals_ref[n], identity) for n in range(ROWS)]
+    maps = [jnp.where(n > place, decoded_map(totals_ref, n), identity) for n in range(ROWS)]
     pairs = [joined(maps[n], maps[n + 1]) for n in (2, 4, 6)]
     front = joined(maps[1], pairs[0])
     back = joined(pairs[1], pairs[2])
     state = product(split(back[HEAD_DIM:]), split(front[:HEAD_DIM])) + front[HEAD_DIM:]
-    states_ref[ROWS - 1] = state
+    states = [state]
     state = split(state)
-    for n in range(ROWS - 1):
+    for n in reversed(range(ROWS - 1)):
         moved = product(state, split(suffix_ref[n, :HEAD_DIM, :]))
-        states_ref[n] = moved + suffix_ref[n, HEAD_DIM:, :]
+        states.append(moved + suffix_ref[n, HEAD_DIM:, :])
+    for n, part in enumerate(reversed(states)):
+        carrier, scale = coded(part)
+        states_ref[n, :HALF, :] = carrier
+        states_ref[n, HALF:, :] = notes_of(scale)
 
 
 def result_kernel(gain_ref, own_ref, state_ref, out_ref):
-    high, low = split(state_ref[0])
-
     def against(left, right):
         return lax.dot_general(
             left, right, (((1,), (1,)), ((), ())), preferred_element_type=F32
         )
 
-    moved = against(gain_ref[0], jnp.concatenate([high, high], axis=1))
-    moved = moved + against(gain_ref[0, :, :HEAD_DIM], low)
-    out_ref[...] = (own_ref[0] + moved).astype(BF16)
-
-
-def per_head(*shape):
-    return pl.BlockSpec((1,) + shape, lambda h: (h,) + (0,) * len(shape))
+    for h in range(gain_ref.shape[0]):
+        parts = [
+            decoded(state_ref[n, :HALF, :], state_ref[n, HALF:, :].astype(F32)[0:1])
+            for n in (2 * h, 2 * h + 1)
+        ]
+        high, low = split(jnp.concatenate(parts, axis=0))
+        moved = against(gain_ref[h], jnp.concatenate([high, high], axis=1))
+        moved = moved + against(gain_ref[h, :, :HEAD_DIM], low)
+        out_ref[:, h * HEAD_DIM : (h + 1) * HEAD_DIM] = (own_ref[h] + moved).astype(BF16)
 
 
 def params():
-    return pltpu.CompilerParams(vmem_limit_bytes=48 * 1024 * 1024)
-
-
-def whole(kernel, out_shapes, *args, scalar=False):
-    vmem = pl.BlockSpec(memory_space=pltpu.VMEM)
-    specs = [vmem] * len(args)
-    if scalar:
-        specs[0] = pl.BlockSpec(memory_space=pltpu.SMEM)
+    return pltpu.CompilerParams(vmem_limit_bytes=40 * 1024 * 1024)
+
+
+def in_vmem(shape, dtype=F32):
+    return pl.BlockSpec(memory_space=pltpu.VMEM), jax.ShapeDtypeStruct(shape, dtype)
+
+
+def in_hbm(shape, dtype=F32):
+    return pl.BlockSpec(memory_space=pl.ANY), pltpu.HBM(shape, dtype)
+
+
+def whole(kernel, outs, *args, first=pltpu.VMEM, scratch=()):
+    specs = [pl.BlockSpec(memory_space=pltpu.VMEM)] * len(args)
+    specs[0] = pl.BlockSpec(memory_space=first)
     return pl.pallas_call(
         kernel,
-        out_shape=[jax.ShapeDtypeStruct(shape, F32) for shape in out_shapes],
         in_specs=specs,
-        out_specs=[vmem] * len(out_shapes),
+        out_specs=[spec for spec, _ in outs],
+        out_shape=[shape for _, shape in outs],
+        scratch_shapes=scratch,
         compiler_params=params(),
     )(*args)
 
 
 def local(queries, keys, decay_log, write_rate, output_grad):
     heads, tokens = write_rate.shape
-    gathered = lax.all_to_all(output_grad, "head", split_axis=1, concat_axis=0, tiled=True)
+    devices = lax.axis_size("head")
+    width = heads * HEAD_DIM
+    part = devices // 2
+    pieces = pl.pallas_call(
+        pieces_kernel,
+        grid=(2,),
+        in_specs=[pl.BlockSpec((tokens // devices, part * width), lambda s: (0, s))],
+        out_specs=pl.BlockSpec((part, tokens // devices, width), lambda s: (s, 0, 0)),
+        out_shape=pltpu.HBM((devices, tokens // devices, width), BF16),
+        compiler_params=params(),
+    )(pltpu.with_memory_space_constraint(output_grad, pltpu.HBM))
+    gathered = lax.all_to_all(pieces, "head", 0, 0, tiled=True).reshape(tokens, width)
     rates = write_rate.reshape(heads, 1, tokens)
-    lanes = pl.BlockSpec((tokens, HEAD_DIM), lambda h: (0, h))
-    square = per_head(HEAD_DIM, HEAD_DIM)
-    tall = per_head(tokens, HEAD_DIM)
-
-    def shape(*dims, dtype=F32):
-        return jax.ShapeDtypeStruct((heads,) + dims, dtype)
-
-    trans, lift, carry, reply, steps, sources = pl.pallas_call(
+
+    def blocks(count, *dims):
+        return pl.BlockSpec((count,) + dims, lambda s: (s,) + (0,) * len(dims))
+
+    def lanes(count):
+        return pl.BlockSpec((tokens, count * HEAD_DIM), lambda s: (0, s))
+
+    def by_heads(kernel, count, args, in_specs, outs):
+        return pl.pallas_call(
+            kernel,
+            grid=(heads // count,),
+            in_specs=in_specs,
+            out_specs=[spec for spec, _ in outs],
+            out_shape=[shape for _, shape in outs],
+            compiler_params=params(),
+        )(*args)
+
+    def out(count, *dims, dtype=F32):
+        return blocks(count, *dims), jax.ShapeDtypeStruct((heads,) + dims, dtype)
+
+    tall_shape = (heads, tokens, HEAD_DIM)
+    trans, lift, carry, reply, steps, sources = whole(
         maps_kernel,
-        grid=(heads,),
-        in_specs=[lanes, lanes, lanes, per_head(1, tokens)],
-        out_specs=[square, per_head(HEAD_DIM, tokens), tall, tall, tall, tall],
-        out_shape=[
-            shape(HEAD_DIM, HEAD_DIM), shape(HEAD_DIM, tokens),
-            shape(tokens, HEAD_DIM), shape(tokens, HEAD_DIM),
-            shape(tokens, HEAD_DIM), shape(tokens, HEAD_DIM),
-        ],
-        compiler_params=params(),
-    )(queries, keys, decay_log, rates)
-    packet = pl.pallas_call(
-        packet_kernel,
-        grid=(heads,),
-        in_specs=[square, per_head(HEAD_DIM, tokens), lanes],
-        out_specs=pl.BlockSpec((2, PACKET, HEAD_DIM), lambda h: (h, 0, 0)),
-        out_shape=jax.ShapeDtypeStruct((2 * heads, PACKET, HEAD_DIM), F32),
-        compiler_params=params(),
-    )(trans, lift, gathered)
+        [in_vmem((heads, HEAD_DIM, HEAD_DIM)), in_vmem((heads, HEAD_DIM, tokens))]
+        + [in_hbm(tall_shape)] * 4,
+        queries,
+        keys,
+        decay_log,
+        rates,
+        scratch=[pltpu.VMEM(tall_shape, F32)] * 4 + [pltpu.SemaphoreType.DMA((4,))],
+    )
+    full, half = (ROWS, PACKET + NOTES, HEAD_DIM), (ROWS, HALF + NOTES, HEAD_DIM)
+    (packet,) = whole(packet_kernel, [in_vmem(full, BF16)], trans, lift, gathered)
     maps = lax.all_to_all(packet, "y", 0, 0, tiled=True)
-    gain, own = pl.pallas_call(
+    tall = blocks(1, tokens, HEAD_DIM)
+    gain, own = by_heads(
         answer_kernel,
-        grid=(heads,),
-        in_specs=[tall, tall, tall, tall, per_head(1, tokens), lanes],
-        out_specs=[per_head(tokens, 2 * HEAD_DIM), tall],
-        out_shape=[shape(tokens, 2 * HEAD_DIM, dtype=BF16), shape(tokens, HEAD_DIM)],
-        compiler_params=params(),
-    )(carry, reply, steps, sources, rates, gathered)
-    total, some = whole(row_kernel, [(ROWS, PACKET, HEAD_DIM), (3, PACKET, HEAD_DIM)], maps)
+        1,
+        tuple(
+            pltpu.with_memory_space_constraint(late, pltpu.HBM)
+            for late in (carry, reply, steps, sources)
+        )
+        + (rates, gathered),
+        [tall, tall, tall, tall, blocks(1, 1, tokens), lanes(1)],
+        [out(1, tokens, 2 * HEAD_DIM, dtype=BF16), out(1, tokens, HEAD_DIM)],
+    )
+    total, some = whole(row_kernel, [in_vmem(full, BF16), in_vmem((3, PACKET, HEAD_DIM))], maps)
     totals = lax.all_to_all(total, "z", 0, 0, tiled=True)
-    (suffix,) = whole(suffix_kernel, [(ROWS - 1, PACKET, HEAD_DIM)], maps, some)
+    (suffix,) = whole(suffix_kernel, [in_vmem((ROWS - 1, PACKET, HEAD_DIM))], maps, some)
+    totals, gain, own = lax.optimization_barrier((totals, gain, own))
     place = lax.axis_index("z").astype(jnp.int32).reshape(1)
-    (states,) = whole(
-        state_kernel, [(ROWS, HALF, HEAD_DIM)], place, totals, suffix, scalar=True
-    )
-    states = lax.all_to_all(states, "y", 0, 0, tiled=True).reshape(heads, HEAD_DIM, HEAD_DIM)
-    return pl.pallas_call(
-        result_kernel,
-        grid=(heads,),
-        in_specs=[per_head(tokens, 2 * HEAD_DIM), tall, square],
-        out_specs=lanes,
-        out_shape=jax.ShapeDtypeStruct((tokens, heads * HEAD_DIM), BF16),
-        compiler_params=params(),
-    )(gain, own, states)
+    (states,) = whole(state_kernel, [in_vmem(half, BF16)], place, totals, suffix, first=pltpu.SMEM)
+    states = lax.all_to_all(states, "y", 0, 0, tiled=True)
+    (result,) = whole(result_kernel, [in_vmem((tokens, width), BF16)], gain, own, states)
+    return result
 
 
 def solution(mesh):

time: 111 us -> 81.1 us (0.73)
  the two profiles are of different devices: /device:TPU:1 before, /device:TPU:2 now
where the time goes in v1:
time: 81.1 us; the launch traced here: 80.6 us
  blocking collectives  30.2 us (37%)
  Pallas kernels  21.2 us (26%)
  starting transfers between devices  19.5 us (24%)
  waiting for transfers between devices  7.59 us (9%)
  local copies, waits for them, and re-layouts  2.02 us (2%)
    all_to_all x1, blocking collectives, local(): maps = lax.all_to_all(packet, 'y', 0, 0, tiled=True)  18.4 us
    pallas_call x6, Pallas kernels, whole(): pl.pallas_call(kernel, in_specs=specs, out_specs=[spec for spec, _ in out...  14.1 us
    all_to_all x1, blocking collectives, local(): states = lax.all_to_all(states, 'y', 0, 0, tiled=True)  11.8 us
    all_to_all x1, starting transfers between devices, local(): totals = lax.all_to_all(total, 'z', 0, 0, tiled=True)  10.1 us
    all_to_all x1, starting transfers between devices, local(): lax.all_to_all(pieces, 'head', 0, 0, tiled=True).reshape(tokens, width)  9.44 us
    all_to_all x1, waiting for transfers between devices, local(): totals = lax.all_to_all(total, 'z', 0, 0, tiled=True)  7.59 us
    pallas_call x1, Pallas kernels, by_heads(): pl.pallas_call(kernel, grid=(heads // count,), in_specs=in_specs, out_spe...  5.26 us
    unnamed x12, local copies, waits for them, and re-layouts  2.02 us
  transfers between devices with their start and end apart: 2, of which 1 were waited for; matrix products, arithmetic and copies ran while one was open for 0% of the time, Pallas kernels for 17%

profile of v1, /device:TPU:2, one launch (start us, length us, event | category | flops | bytes accessed | tf_op | source)
XLA Modules:
  0.0 80.6 jit_solution(107465291026849105)
XLA Ops:
  0.0 0.0 copy-start
  0.0 1.8 %shard_map.56 = bf16[8,64,512]{2,1,0:T(8,128)(2,1)} custom-call(bf16[64,4096]{1,0:T(8,128)(2,1)} %grads_ref.1), custom_call_target="tpu_custom_call" | custom-call | tf_op jit(solution)/shard_map/pallas_call | solution.py:393
  1.8 0.0 copy-start.5
  1.9 0.0 copy-start.3
  1.9 9.4 %all-to-all-start = ((bf16[8,64,512]{2,1,0:T(8,128)(2,1)}), bf16[8,64,512]{2,1,0:T(8,128)(2,1)S(1)}, u32[]{:S(2)}, u32[]{:S(2)}) async-start(bf16[8,64,512]{2,1,0:T(8,128)(2,1)} %shard_map.56), calls=%async_computation | async-start | bytes 1048576 | tf_op jit(solution)/shard_map/all_to_all | solution.py:401
  11.3 0.0 copy-done.5
  11.3 0.0 copy-done
  11.3 0.0 copy-done.3
  11.3 0.0 copy-start.4
  11.3 1.0 %copy-done.4 = bf16[512,512]{1,0:T(8,128)(2,1)S(1)} copy-done((bf16[512,512]{1,0:T(8,128)(2,1)S(1)}, bf16[512,512]{1,0:T(8,128)(2,1)}, u32[]{:S(2)}) %copy-start.4) | copy-done | bytes 524312
  12.4 8.1 %shard_map.55 = (f32[4,128,128]{2,1,0:T(8,128)S(1)}, f32[4,128,512]{2,1,0:T(8,128)S(1)}, f32[4,512,128]{2,1,0:T(8,128)}, f32[4,512,128]{2,1,0:T(8,128)}, f32[4,512,128]{2,1,0:T(8,128)}, /*index=5*/f32[4,512,128]{2,1,0:T(8,128)}) custom-call(bf16[512,512]{1,0:T(8,128)(2,1)S(1)} %copy-done.3, bf16[512,512]{1,0:T(8,128)(2,1)S(1)} %copy-done.4, ...), custom_call_target="tpu_custom_call" | custom-call | tf_op jit(solution)/shard_map/pallas_call | solution.py:378
  20.5 0.0 all-to-all-done
  20.5 0.8 %shard_map.57 = bf16[8,208,128]{2,1,0:T(8,128)(2,1)S(1)} custom-call(f32[4,128,128]{2,1,0:T(8,128)S(1)} %get-tuple-element.18.trans_ref, f32[4,128,512]{2,1,0:T(8,128)S(1)} %get-tuple-element.19.lift_ref, bf16[512,512]{1,0:T(8,128)(2,1)S(1)} %bitcast.2), custom_call_target="tpu_custom_call" | custom-call | tf_op jit(solution)/shard_map/pallas_call | solution.py:378
  21.4 18.4 %all_to_all.20.maps_ref = bf16[8,208,128]{2,1,0:T(8,128)(2,1)S(1)} all-to-all(bf16[8,208,128]{2,1,0:T(8,128)(2,1)S(1)} %shard_map.57), channel_id=1, replica_groups=mesh['z'=8,'y'=8,'head'=8] {'y'}, dimensions={0} | all-to-all | bytes 851968 | tf_op jit(solution)/shard_map/all_to_all | solution.py:436
  39.7 1.8 %shard_map.58 = (bf16[8,208,128]{2,1,0:T(8,128)(2,1)}, f32[3,192,128]{2,1,0:T(8,128)S(1)}) custom-call(bf16[8,208,128]{2,1,0:T(8,128)(2,1)S(1)} %all_to_all.20.maps_ref), custom_call_target="tpu_custom_call" | custom-call | tf_op jit(solution)/shard_map/pallas_call | solution.py:378
  41.6 10.1 %all-to-all-start.2 = ((bf16[8,208,128]{2,1,0:T(8,128)(2,1)}), bf16[8,208,128]{2,1,0:T(8,128)(2,1)S(1)}, u32[]{:S(2)}, u32[]{:S(2)}) async-start(bf16[8,208,128]{2,1,0:T(8,128)(2,1)} %get-tuple-element.20), calls=%async_computation.2 | async-start | bytes 851968 | tf_op jit(solution)/shard_map/all_to_all | solution.py:450
  51.6 5.3 %shard_map.59 = (bf16[4,512,256]{2,1,0:T(8,128)(2,1)S(1)}, f32[4,512,128]{2,1,0:T(8,128)S(1)}) custom-call(f32[4,512,128]{2,1,0:T(8,128)} %get-tuple-element.21.carry_ref, f32[4,512,128]{2,1,0:T(8,128)} %get-tuple-element.22.reply_ref, f32[4,512,128]{2,1,0:T(8,128)} %get-tuple-element.23.step_ref, f32[4,512,128]{2,1,0:T(8,128)} %get-tuple-element.24.source_ref, ...), custom_call_target="tpu_custom_call" | custom-call | tf_op jit(solution)/shard_map/pallas_call | solution.py:411
  56.9 0.0 copy-start.1
  56.9 1.0 %copy-done.1 = f32[4,512,128]{2,1,0:T(8,128)} copy-done((f32[4,512,128]{2,1,0:T(8,128)}, f32[4,512,128]{2,1,0:T(8,128)S(1)}, u32[]{:S(2)}) %copy-start.1) | copy-done | bytes 1048600
  57.9 0.5 shard_map.60.suffix_ref
  58.4 7.6 %all-to-all-done.2.totals_ref = bf16[8,208,128]{2,1,0:T(8,128)(2,1)S(1)} async-done(((bf16[8,208,128]{2,1,0:T(8,128)(2,1)}), bf16[8,208,128]{2,1,0:T(8,128)(2,1)S(1)}, u32[]{:S(2)}, u32[]{:S(2)}) %all-to-all-start.2) | async-done | bytes 426016 | tf_op jit(solution)/shard_map/all_to_all | solution.py:450
  66.0 0.0 copy-start.2
  66.0 1.3 %shard_map.61 = bf16[8,80,128]{2,1,0:T(8,128)(2,1)S(1)} custom-call(s32[1]{0:T(128)} %bitcast.1.place_ref, bf16[8,208,128]{2,1,0:T(8,128)(2,1)S(1)} %all-to-all-done.2.totals_ref, f32[7,192,128]{2,1,0:T(8,128)S(1)} %shard_map.60.suffix_ref), custom_call_target="tpu_custom_call" | custom-call | tf_op jit(solution)/shard_map/pallas_call | solution.py:378
  67.3 11.8 %all_to_all.21.state_ref = bf16[8,80,128]{2,1,0:T(8,128)(2,1)S(1)} all-to-all(bf16[8,80,128]{2,1,0:T(8,128)(2,1)S(1)} %shard_map.61), channel_id=1, replica_groups=mesh['z'=8,'y'=8,'head'=8] {'y'}, dimensions={0} | all-to-all | bytes 327680 | tf_op jit(solution)/shard_map/all_to_all | solution.py:455
  79.1 0.0 copy-done.2
  79.1 1.5 %shard_map.62 = bf16[512,512]{1,0:T(8,128)(2,1)} custom-call(bf16[4,512,256]{2,1,0:T(8,128)(2,1)S(1)} %get-tuple-element.27.gain_ref, f32[4,512,128]{2,1,0:T(8,128)S(1)} %copy-done.2, bf16[8,80,128]{2,1,0:T(8,128)(2,1)S(1)} %all_to_all.21.state_ref), custom_call_target="tpu_custom_call" | custom-call | tf_op jit(solution)/shard_map/pallas_call | solution.py:378
  (1 shorter events, 0.0 us)
Async XLA Ops:
  0.0 11.3 %copy-start = (f32[512,512]{1,0:T(8,128)S(1)}, f32[512,512]{1,0:T(8,128)}, u32[]{:S(2)}) copy-start(f32[512,512]{1,0:T(8,128)} %decay_ref.1) | copy-start | bytes 3145732
  1.8 9.4 %copy-start.5 = (f32[4,512]{1,0:T(4,128)S(1)}, f32[4,512]{1,0:T(4,128)}, u32[]{:S(2)}) copy-start(f32[4,512]{1,0:T(4,128)} %param.8) | copy-start | bytes 24580
  1.9 9.5 %copy-start.3 = (bf16[512,512]{1,0:T(8,128)(2,1)S(1)}, bf16[512,512]{1,0:T(8,128)(2,1)}, u32[]{:S(2)}) copy-start(bf16[512,512]{1,0:T(8,128)(2,1)} %queries_ref.1) | copy-start | bytes 1572868
  1.9 18.7 %all-to-all-start = ((bf16[8,64,512]{2,1,0:T(8,128)(2,1)}), bf16[8,64,512]{2,1,0:T(8,128)(2,1)S(1)}, u32[]{:S(2)}, u32[]{:S(2)}) async-start(bf16[8,64,512]{2,1,0:T(8,128)(2,1)} %shard_map.56), calls=%async_computation | async-start | bytes 1048576 | tf_op jit(solution)/shard_map/all_to_all | solution.py:401
  11.3 1.0 %copy-start.4 = (bf16[512,512]{1,0:T(8,128)(2,1)S(1)}, bf16[512,512]{1,0:T(8,128)(2,1)}, u32[]{:S(2)}) copy-start(bf16[512,512]{1,0:T(8,128)(2,1)} %keys_ref.1) | copy-start | bytes 1572868
  41.6 24.4 %all-to-all-start.2 = ((bf16[8,208,128]{2,1,0:T(8,128)(2,1)}), bf16[8,208,128]{2,1,0:T(8,128)(2,1)S(1)}, u32[]{:S(2)}, u32[]{:S(2)}) async-start(bf16[8,208,128]{2,1,0:T(8,128)(2,1)} %get-tuple-element.20), calls=%async_computation.2 | async-start | bytes 851968 | tf_op jit(solution)/shard_map/all_to_all | solution.py:450
  56.9 1.0 %copy-start.1 = (f32[4,512,128]{2,1,0:T(8,128)}, f32[4,512,128]{2,1,0:T(8,128)S(1)}, u32[]{:S(2)}) copy-start(f32[4,512,128]{2,1,0:T(8,128)S(1)} %get-tuple-element.28.own_ref) | copy-start | bytes 3145732
  66.0 13.1 %copy-start.2 = (f32[4,512,128]{2,1,0:T(8,128)S(1)}, f32[4,512,128]{2,1,0:T(8,128)}, u32[]{:S(2)}) copy-start(f32[4,512,128]{2,1,0:T(8,128)} %copy-done.1) | copy-start | bytes 3145732

commit v2 on v1

--- a/solution.py
+++ b/solution.py
@@ -232,10 +232,18 @@
     return jnp.concatenate([jnp.where(row == col, diagonal, trans), source], axis=0)
 
 
-def pieces_kernel(grads_ref, pieces_ref):
+def pieces_kernel(grads_ref, pieces_ref, sems):
     count, _, width = pieces_ref.shape
-    for n in range(count):
-        pieces_ref[n] = grads_ref[:, n * width : (n + 1) * width]
+    copies = [
+        pltpu.make_async_copy(
+            grads_ref.at[:, n * width : (n + 1) * width], pieces_ref.at[n], sems.at[n]
+        )
+        for n in range(count)
+    ]
+    for copy in copies:
+        copy.start()
+    for copy in copies:
+        copy.wait()
 
 
 def packet_kernel(trans_ref, lift_ref, grads_ref, packet_ref):
@@ -355,8 +363,10 @@
             for n in (2 * h, 2 * h + 1)
         ]
         high, low = split(jnp.concatenate(parts, axis=0))
-        moved = against(gain_ref[h], jnp.concatenate([high, high], axis=1))
-        moved = moved + against(gain_ref[h, :, :HEAD_DIM], low)
+        upper = jnp.concatenate([high, high], axis=1)
+        lower = jnp.concatenate([low, jnp.zeros_like(low)], axis=1)
+        moved = against(gain_ref[h], jnp.concatenate([upper, lower], axis=0))
+        moved = moved[:, :HEAD_DIM] + moved[:, HEAD_DIM:]
         out_ref[:, h * HEAD_DIM : (h + 1) * HEAD_DIM] = (own_ref[h] + moved).astype(BF16)
 
 
@@ -389,15 +399,13 @@
     heads, tokens = write_rate.shape
     devices = lax.axis_size("head")
     width = heads * HEAD_DIM
-    part = devices // 2
-    pieces = pl.pallas_call(
+    (pieces,) = whole(
         pieces_kernel,
-        grid=(2,),
-        in_specs=[pl.BlockSpec((tokens // devices, part * width), lambda s: (0, s))],
-        out_specs=pl.BlockSpec((part, tokens // devices, width), lambda s: (s, 0, 0)),
-        out_shape=pltpu.HBM((devices, tokens // devices, width), BF16),
-        compiler_params=params(),
-    )(pltpu.with_memory_space_constraint(output_grad, pltpu.HBM))
+        [in_vmem((devices, tokens // devices, width), BF16)],
+        pltpu.with_memory_space_constraint(output_grad, pltpu.HBM),
+        first=pltpu.HBM,
+        scratch=[pltpu.SemaphoreType.DMA((devices,))],
+    )
     gathered = lax.all_to_all(pieces, "head", 0, 0, tiled=True).reshape(tokens, width)
     rates = write_rate.reshape(heads, 1, tokens)
 

time: 81.1 us -> 81.1 us (level)
    pallas_call x1 -> x0, Pallas kernels: 1.84 us -> none  [local(): pl.pallas_call(pieces_kernel, grid=(2,), in_specs=[pl.BlockSpec((tokens /...]
    pallas_call x6 -> x7, Pallas kernels: 14.1 us -> 15.9 us  [whole(): pl.pallas_call(kernel, in_specs=specs, out_specs=[spec for spec, _ in out...]
where the time goes in v2:
time: 81.1 us; the launch traced here: 80.6 us
  blocking collectives  30.2 us (37%)
  Pallas kernels  21.2 us (26%)
  starting transfers between devices  19.5 us (24%)
  waiting for transfers between devices  7.58 us (9%)
  local copies, waits for them, and re-layouts  2.03 us (3%)
    all_to_all x1, blocking collectives, local(): maps = lax.all_to_all(packet, 'y', 0, 0, tiled=True)  18.4 us
    pallas_call x7, Pallas kernels, whole(): pl.pallas_call(kernel, in_specs=specs, out_specs=[spec for spec, _ in out...  15.9 us
    all_to_all x1, blocking collectives, local(): states = lax.all_to_all(states, 'y', 0, 0, tiled=True)  11.8 us
    all_to_all x1, starting transfers between devices, local(): totals = lax.all_to_all(total, 'z', 0, 0, tiled=True)  10.1 us
    all_to_all x1, starting transfers between devices, local(): lax.all_to_all(pieces, 'head', 0, 0, tiled=True).reshape(tokens, width)  9.45 us
    all_to_all x1, waiting for transfers between devices, local(): totals = lax.all_to_all(total, 'z', 0, 0, tiled=True)  7.58 us
    pallas_call x1, Pallas kernels, by_heads(): pl.pallas_call(kernel, grid=(heads // count,), in_specs=in_specs, out_spe...  5.26 us
    unnamed x12, local copies, waits for them, and re-layouts  2.02 us
  transfers between devices with their start and end apart: 2, of which 1 were waited for; matrix products, arithmetic and copies ran while one was open for 0% of the time, Pallas kernels for 17%

profile of v2, /device:TPU:2, one launch (start us, length us, event | category | flops | bytes accessed | tf_op | source)
XLA Modules:
  0.0 80.6 jit_solution(1526652394654940999)
XLA Ops:
  0.0 0.0 copy-start
  0.0 2.0 %shard_map.56 = bf16[8,64,512]{2,1,0:T(8,128)(2,1)} custom-call(bf16[64,4096]{1,0:T(8,128)(2,1)} %grads_ref.1), custom_call_target="tpu_custom_call" | custom-call | tf_op jit(solution)/shard_map/pallas_call | solution.py:388
  2.0 0.0 copy-start.5
  2.0 0.0 copy-start.3
  2.0 9.5 %all-to-all-start = ((bf16[8,64,512]{2,1,0:T(8,128)(2,1)}), bf16[8,64,512]{2,1,0:T(8,128)(2,1)S(1)}, u32[]{:S(2)}, u32[]{:S(2)}) async-start(bf16[8,64,512]{2,1,0:T(8,128)(2,1)} %shard_map.56), calls=%async_computation | async-start | bytes 1048576 | tf_op jit(solution)/shard_map/all_to_all | solution.py:409
  11.5 0.0 copy-done.5
  11.5 0.0 copy-done
  11.5 0.0 copy-done.3
  11.5 0.0 copy-start.4
  11.5 1.0 %copy-done.4 = bf16[512,512]{1,0:T(8,128)(2,1)S(1)} copy-done((bf16[512,512]{1,0:T(8,128)(2,1)S(1)}, bf16[512,512]{1,0:T(8,128)(2,1)}, u32[]{:S(2)}) %copy-start.4) | copy-done | bytes 524312
  12.6 8.1 %shard_map.55 = (f32[4,128,128]{2,1,0:T(8,128)S(1)}, f32[4,128,512]{2,1,0:T(8,128)S(1)}, f32[4,512,128]{2,1,0:T(8,128)}, f32[4,512,128]{2,1,0:T(8,128)}, f32[4,512,128]{2,1,0:T(8,128)}, /*index=5*/f32[4,512,128]{2,1,0:T(8,128)}) custom-call(bf16[512,512]{1,0:T(8,128)(2,1)S(1)} %copy-done.3, bf16[512,512]{1,0:T(8,128)(2,1)S(1)} %copy-done.4, ...), custom_call_target="tpu_custom_call" | custom-call | tf_op jit(solution)/shard_map/pallas_call | solution.py:388
  20.7 0.0 all-to-all-done
  20.7 0.8 %shard_map.57 = bf16[8,208,128]{2,1,0:T(8,128)(2,1)S(1)} custom-call(f32[4,128,128]{2,1,0:T(8,128)S(1)} %get-tuple-element.18.trans_ref, f32[4,128,512]{2,1,0:T(8,128)S(1)} %get-tuple-element.19.lift_ref, bf16[512,512]{1,0:T(8,128)(2,1)S(1)} %bitcast.2), custom_call_target="tpu_custom_call" | custom-call | tf_op jit(solution)/shard_map/pallas_call | solution.py:388
  21.5 18.4 %all_to_all.20.maps_ref = bf16[8,208,128]{2,1,0:T(8,128)(2,1)S(1)} all-to-all(bf16[8,208,128]{2,1,0:T(8,128)(2,1)S(1)} %shard_map.57), channel_id=1, replica_groups=mesh['z'=8,'y'=8,'head'=8] {'y'}, dimensions={0} | all-to-all | bytes 851968 | tf_op jit(solution)/shard_map/all_to_all | solution.py:444
  39.9 1.8 %shard_map.58 = (bf16[8,208,128]{2,1,0:T(8,128)(2,1)}, f32[3,192,128]{2,1,0:T(8,128)S(1)}) custom-call(bf16[8,208,128]{2,1,0:T(8,128)(2,1)S(1)} %all_to_all.20.maps_ref), custom_call_target="tpu_custom_call" | custom-call | tf_op jit(solution)/shard_map/pallas_call | solution.py:388
  41.7 10.1 %all-to-all-start.2 = ((bf16[8,208,128]{2,1,0:T(8,128)(2,1)}), bf16[8,208,128]{2,1,0:T(8,128)(2,1)S(1)}, u32[]{:S(2)}, u32[]{:S(2)}) async-start(bf16[8,208,128]{2,1,0:T(8,128)(2,1)} %get-tuple-element.20), calls=%async_computation.2 | async-start | bytes 851968 | tf_op jit(solution)/shard_map/all_to_all | solution.py:458
  51.8 5.3 %shard_map.59 = (bf16[4,512,256]{2,1,0:T(8,128)(2,1)S(1)}, f32[4,512,128]{2,1,0:T(8,128)S(1)}) custom-call(f32[4,512,128]{2,1,0:T(8,128)} %get-tuple-element.21.carry_ref, f32[4,512,128]{2,1,0:T(8,128)} %get-tuple-element.22.reply_ref, f32[4,512,128]{2,1,0:T(8,128)} %get-tuple-element.23.step_ref, f32[4,512,128]{2,1,0:T(8,128)} %get-tuple-element.24.source_ref, ...), custom_call_target="tpu_custom_call" | custom-call | tf_op jit(solution)/shard_map/pallas_call | solution.py:419
  57.1 0.0 copy-start.1
  57.1 1.0 %copy-done.1 = f32[4,512,128]{2,1,0:T(8,128)} copy-done((f32[4,512,128]{2,1,0:T(8,128)}, f32[4,512,128]{2,1,0:T(8,128)S(1)}, u32[]{:S(2)}) %copy-start.1) | copy-done | bytes 1048600
  58.1 0.5 shard_map.60.suffix_ref
  58.6 7.6 %all-to-all-done.2.totals_ref = bf16[8,208,128]{2,1,0:T(8,128)(2,1)S(1)} async-done(((bf16[8,208,128]{2,1,0:T(8,128)(2,1)}), bf16[8,208,128]{2,1,0:T(8,128)(2,1)S(1)}, u32[]{:S(2)}, u32[]{:S(2)}) %all-to-all-start.2) | async-done | bytes 426016 | tf_op jit(solution)/shard_map/all_to_all | solution.py:458
  66.2 0.0 copy-start.2
  66.2 1.3 %shard_map.61 = bf16[8,80,128]{2,1,0:T(8,128)(2,1)S(1)} custom-call(s32[1]{0:T(128)} %bitcast.1.place_ref, bf16[8,208,128]{2,1,0:T(8,128)(2,1)S(1)} %all-to-all-done.2.totals_ref, f32[7,192,128]{2,1,0:T(8,128)S(1)} %shard_map.60.suffix_ref), custom_call_target="tpu_custom_call" | custom-call | tf_op jit(solution)/shard_map/pallas_call | solution.py:388
  67.4 11.8 %all_to_all.21.state_ref = bf16[8,80,128]{2,1,0:T(8,128)(2,1)S(1)} all-to-all(bf16[8,80,128]{2,1,0:T(8,128)(2,1)S(1)} %shard_map.61), channel_id=1, replica_groups=mesh['z'=8,'y'=8,'head'=8] {'y'}, dimensions={0} | all-to-all | bytes 327680 | tf_op jit(solution)/shard_map/all_to_all | solution.py:463
  79.2 0.0 copy-done.2
  79.3 1.4 %shard_map.62 = bf16[512,512]{1,0:T(8,128)(2,1)} custom-call(bf16[4,512,256]{2,1,0:T(8,128)(2,1)S(1)} %get-tuple-element.27.gain_ref, f32[4,512,128]{2,1,0:T(8,128)S(1)} %copy-done.2, bf16[8,80,128]{2,1,0:T(8,128)(2,1)S(1)} %all_to_all.21.state_ref), custom_call_target="tpu_custom_call" | custom-call | tf_op jit(solution)/shard_map/pallas_call | solution.py:388
  (1 shorter events, 0.0 us)
Async XLA Ops:
  0.0 11.5 %copy-start = (f32[512,512]{1,0:T(8,128)S(1)}, f32[512,512]{1,0:T(8,128)}, u32[]{:S(2)}) copy-start(f32[512,512]{1,0:T(8,128)} %decay_ref.1) | copy-start | bytes 3145732
  2.0 9.5 %copy-start.5 = (f32[4,512]{1,0:T(4,128)S(1)}, f32[4,512]{1,0:T(4,128)}, u32[]{:S(2)}) copy-start(f32[4,512]{1,0:T(4,128)} %param.8) | copy-start | bytes 24580
  2.0 9.5 %copy-start.3 = (bf16[512,512]{1,0:T(8,128)(2,1)S(1)}, bf16[512,512]{1,0:T(8,128)(2,1)}, u32[]{:S(2)}) copy-start(bf16[512,512]{1,0:T(8,128)(2,1)} %queries_ref.1) | copy-start | bytes 1572868
  2.0 18.7 %all-to-all-start = ((bf16[8,64,512]{2,1,0:T(8,128)(2,1)}), bf16[8,64,512]{2,1,0:T(8,128)(2,1)S(1)}, u32[]{:S(2)}, u32[]{:S(2)}) async-start(bf16[8,64,512]{2,1,0:T(8,128)(2,1)} %shard_map.56), calls=%async_computation | async-start | bytes 1048576 | tf_op jit(solution)/shard_map/all_to_all | solution.py:409
  11.5 1.0 %copy-start.4 = (bf16[512,512]{1,0:T(8,128)(2,1)S(1)}, bf16[512,512]{1,0:T(8,128)(2,1)}, u32[]{:S(2)}) copy-start(bf16[512,512]{1,0:T(8,128)(2,1)} %keys_ref.1) | copy-start | bytes 1572868
  41.7 24.4 %all-to-all-start.2 = ((bf16[8,208,128]{2,1,0:T(8,128)(2,1)}), bf16[8,208,128]{2,1,0:T(8,128)(2,1)S(1)}, u32[]{:S(2)}, u32[]{:S(2)}) async-start(bf16[8,208,128]{2,1,0:T(8,128)(2,1)} %get-tuple-element.20), calls=%async_computation.2 | async-start | bytes 851968 | tf_op jit(solution)/shard_map/all_to_all | solution.py:458
  57.1 1.0 %copy-start.1 = (f32[4,512,128]{2,1,0:T(8,128)}, f32[4,512,128]{2,1,0:T(8,128)S(1)}, u32[]{:S(2)}) copy-start(f32[4,512,128]{2,1,0:T(8,128)S(1)} %get-tuple-element.28.own_ref) | copy-start | bytes 3145732
  66.2 13.1 %copy-start.2 = (f32[4,512,128]{2,1,0:T(8,128)S(1)}, f32[4,512,128]{2,1,0:T(8,128)}, u32[]{:S(2)}) copy-start(f32[4,512,128]{2,1,0:T(8,128)} %copy-done.1) | copy-start | bytes 3145732

commit v3 on v2

--- a/solution.py
+++ b/solution.py
@@ -98,7 +98,7 @@
 
 def maps_kernel(
     queries_ref, keys_ref, decay_ref, rate_ref,
-    trans_ref, lift_ref, carry_out, reply_out, step_out, source_out,
+    trans_ref, lines_ref, lift_ref, carry_out, reply_out, step_out, source_out,
     carry_ref, reply_ref, step_ref, source_ref, sems,
 ):
     row, col = indices(CHUNK)
@@ -179,9 +179,13 @@
             merged.append((moved[:, :HEAD_DIM], first[1] + pieces))
         parts = merged
     for h, (turned, pieces) in enumerate(parts):
-        trans_ref[h] = turned.T
+        trans_ref[h], lines = coded_trans(turned.T)
+        lines_ref[h, : len(lines), :] = jnp.concatenate(lines, axis=0)
+        width = len(pieces) * CHUNK
         for n, part in enumerate(pieces):
-            lift_ref[h, :, n * CHUNK : (n + 1) * CHUNK] = part
+            high, low = split(part)
+            lift_ref[h, :, n * CHUNK : (n + 1) * CHUNK] = high
+            lift_ref[h, :, width + n * CHUNK : width + (n + 1) * CHUNK] = low
     for copy in copies:
         copy.wait()
 
@@ -246,14 +250,14 @@
         copy.wait()
 
 
-def packet_kernel(trans_ref, lift_ref, grads_ref, packet_ref):
+def packet_kernel(trans_ref, lines_ref, lift_ref, grads_ref, packet_ref):
     for h in range(trans_ref.shape[0]):
         grads = grads_ref[:, h * HEAD_DIM : (h + 1) * HEAD_DIM]
-        source = exact_right(split(lift_ref[h]), grads).T
-        trans, lines = coded_trans(trans_ref[h])
+        source = dot(lift_ref[h], jnp.concatenate([grads, grads], axis=0)).T
+        lines = [lines_ref[h, n : n + 1, :] for n in range(4)]
         for place in range(2):
             half, scale = coded(source[place * HALF : (place + 1) * HALF])
-            packet_ref[2 * h + place, :HEAD_DIM, :] = trans
+            packet_ref[2 * h + place, :HEAD_DIM, :] = trans_ref[h]
             packet_ref[2 * h + place, HEAD_DIM:PACKET, :] = half
             packet_ref[2 * h + place, PACKET:, :] = notes_of(lines[0], scale, *lines[1:])
 
@@ -318,19 +322,24 @@
     some_ref[2] = fours[1]
 
 
-def suffix_kernel(maps_ref, some_ref, suffix_ref):
+def suffix_kernel(maps_ref, some_ref, trans_ref, source_ref):
     pair_second, pair_last, four_last = some_ref[0], some_ref[1], some_ref[2]
-    suffix_ref[6] = decoded_map(maps_ref, 7)
-    suffix_ref[5] = pair_last
-    suffix_ref[4] = joined(decoded_map(maps_ref, 5), pair_last)
-    suffix_ref[3] = four_last
-    suffix_ref[2] = joined(decoded_map(maps_ref, 3), four_last)
     from_second = joined(pair_second, four_last)
-    suffix_ref[1] = from_second
-    suffix_ref[0] = joined(decoded_map(maps_ref, 1), from_second)
-
-
-def state_kernel(place_ref, totals_ref, suffix_ref, states_ref):
+    suffixes = [
+        joined(decoded_map(maps_ref, 1), from_second),
+        from_second,
+        joined(decoded_map(maps_ref, 3), four_last),
+        four_last,
+        joined(decoded_map(maps_ref, 5), pair_last),
+        pair_last,
+        decoded_map(maps_ref, 7),
+    ]
+    for n, part in enumerate(suffixes):
+        trans_ref[n, :HEAD_DIM, :], trans_ref[n, HEAD_DIM:, :] = split(part[:HEAD_DIM])
+        source_ref[n] = part[HEAD_DIM:]
+
+
+def state_kernel(place_ref, totals_ref, trans_ref, source_ref, states_ref):
     place = place_ref[0]
     row = lax.broadcasted_iota(jnp.int32, (PACKET, HEAD_DIM), 0)
     col = lax.broadcasted_iota(jnp.int32, (PACKET, HEAD_DIM), 1)
@@ -343,8 +352,8 @@
     states = [state]
     state = split(state)
     for n in reversed(range(ROWS - 1)):
-        moved = product(state, split(suffix_ref[n, :HEAD_DIM, :]))
-        states.append(moved + suffix_ref[n, HEAD_DIM:, :])
+        moved = product(state, (trans_ref[n, :HEAD_DIM, :], trans_ref[n, HEAD_DIM:, :]))
+        states.append(moved + source_ref[n])
     for n, part in enumerate(reversed(states)):
         carrier, scale = coded(part)
         states_ref[n, :HALF, :] = carrier
@@ -429,9 +438,13 @@
         return blocks(count, *dims), jax.ShapeDtypeStruct((heads,) + dims, dtype)
 
     tall_shape = (heads, tokens, HEAD_DIM)
-    trans, lift, carry, reply, steps, sources = whole(
+    trans, lines, lift, carry, reply, steps, sources = whole(
         maps_kernel,
-        [in_vmem((heads, HEAD_DIM, HEAD_DIM)), in_vmem((heads, HEAD_DIM, tokens))]
+        [
+            in_vmem((heads, HEAD_DIM, HEAD_DIM), BF16),
+            in_vmem((heads, 8, HEAD_DIM)),
+            in_vmem((heads, HEAD_DIM, 2 * tokens), BF16),
+        ]
         + [in_hbm(tall_shape)] * 4,
         queries,
         keys,
@@ -440,7 +453,7 @@
         scratch=[pltpu.VMEM(tall_shape, F32)] * 4 + [pltpu.SemaphoreType.DMA((4,))],
     )
     full, half = (ROWS, PACKET + NOTES, HEAD_DIM), (ROWS, HALF + NOTES, HEAD_DIM)
-    (packet,) = whole(packet_kernel, [in_vmem(full, BF16)], trans, lift, gathered)
+    (packet,) = whole(packet_kernel, [in_vmem(full, BF16)], trans, lines, lift, gathered)
     maps = lax.all_to_all(packet, "y", 0, 0, tiled=True)
     tall = blocks(1, tokens, HEAD_DIM)
     gain, own = by_heads(
@@ -456,10 +469,15 @@
     )
     total, some = whole(row_kernel, [in_vmem(full, BF16), in_vmem((3, PACKET, HEAD_DIM))], maps)
     totals = lax.all_to_all(total, "z", 0, 0, tiled=True)
-    (suffix,) = whole(suffix_kernel, [in_vmem((ROWS - 1, PACKET, HEAD_DIM))], maps, some)
+    suffix = whole(
+        suffix_kernel,
+        [in_vmem((ROWS - 1, 2 * HEAD_DIM, HEAD_DIM), BF16), in_vmem((ROWS - 1, HALF, HEAD_DIM))],
+        maps,
+        some,
+    )
     totals, gain, own = lax.optimization_barrier((totals, gain, own))
     place = lax.axis_index("z").astype(jnp.int32).reshape(1)
-    (states,) = whole(state_kernel, [in_vmem(half, BF16)], place, totals, suffix, first=pltpu.SMEM)
+    (states,) = whole(state_kernel, [in_vmem(half, BF16)], place, totals, *suffix, first=pltpu.SMEM)
     states = lax.all_to_all(states, "y", 0, 0, tiled=True)
     (result,) = whole(result_kernel, [in_vmem((tokens, width), BF16)], gain, own, states)
     return result

time: 81.1 us -> 82.7 us (1.020)
  local copies, waits for them, and re-layouts: 2.03 us -> 3.39 us
    unnamed x12 -> x16, local copies, waits for them, and re-layouts: 2.02 us -> 3.38 us
where the time goes in v3:
time: 82.7 us; the launch traced here: 82.2 us
  blocking collectives  30.2 us (37%)
  Pallas kernels  21.1 us (26%)
  starting transfers between devices  19.5 us (24%)
  waiting for transfers between devices  7.81 us (9%)
  local copies, waits for them, and re-layouts  3.39 us (4%)
    all_to_all x1, blocking collectives, local(): maps = lax.all_to_all(packet, 'y', 0, 0, tiled=True)  18.4 us
    pallas_call x7, Pallas kernels, whole(): pl.pallas_call(kernel, in_specs=specs, out_specs=[spec for spec, _ in out...  15.8 us
    all_to_all x1, blocking collectives, local(): states = lax.all_to_all(states, 'y', 0, 0, tiled=True)  11.8 us
    all_to_all x1, starting transfers between devices, local(): totals = lax.all_to_all(total, 'z', 0, 0, tiled=True)  10.1 us
    all_to_all x1, starting transfers between devices, local(): lax.all_to_all(pieces, 'head', 0, 0, tiled=True).reshape(tokens, width)  9.45 us
    all_to_all x1, waiting for transfers between devices, local(): totals = lax.all_to_all(total, 'z', 0, 0, tiled=True)  7.81 us
    pallas_call x1, Pallas kernels, by_heads(): pl.pallas_call(kernel, grid=(heads // count,), in_specs=in_specs, out_spe...  5.31 us
    unnamed x16, local copies, waits for them, and re-layouts  3.38 us
  transfers between devices with their start and end apart: 2, of which 1 were waited for; matrix products, arithmetic and copies ran while one was open for 0% of the time, Pallas kernels for 17%

profile of v3, /device:TPU:2, one launch (start us, length us, event | category | flops | bytes accessed | tf_op | source)
XLA Modules:
  0.0 82.2 jit_solution(16179048418197984057)
XLA Ops:
  0.0 0.0 copy-start
  0.0 2.0 %shard_map.56 = bf16[8,64,512]{2,1,0:T(8,128)(2,1)} custom-call(bf16[64,4096]{1,0:T(8,128)(2,1)} %grads_ref.1), custom_call_target="tpu_custom_call" | custom-call | tf_op jit(solution)/shard_map/pallas_call | solution.py:397
  2.0 0.0 copy-start.7
  2.0 0.0 copy-start.1
  2.0 9.5 %all-to-all-start = ((bf16[8,64,512]{2,1,0:T(8,128)(2,1)}), bf16[8,64,512]{2,1,0:T(8,128)(2,1)S(1)}, u32[]{:S(2)}, u32[]{:S(2)}) async-start(bf16[8,64,512]{2,1,0:T(8,128)(2,1)} %shard_map.56), calls=%async_computation | async-start | bytes 1048576 | tf_op jit(solution)/shard_map/all_to_all | solution.py:418
  11.5 0.0 copy-done.7
  11.5 0.0 copy-done
  11.5 0.0 copy-done.1
  11.5 0.0 copy-start.2
  11.5 1.0 %copy-done.2 = bf16[512,512]{1,0:T(8,128)(2,1)S(1)} copy-done((bf16[512,512]{1,0:T(8,128)(2,1)S(1)}, bf16[512,512]{1,0:T(8,128)(2,1)}, u32[]{:S(2)}) %copy-start.2) | copy-done | bytes 524312
  12.6 8.3 %shard_map.55 = (bf16[4,128,128]{2,1,0:T(8,128)(2,1)S(1)}, f32[4,8,128]{2,1,0:T(8,128)S(1)}, bf16[4,128,1024]{2,1,0:T(8,128)(2,1)S(1)}, f32[4,512,128]{2,1,0:T(8...) custom-call(bf16[512,512]{1,0:T(8,128)(2,1)S(1)} %copy-done.1, ...), custom_call_target="tpu_custom_call" | custom-call | tf_op jit(solution)/shard_map/pallas_call | solution.py:397
  20.8 0.0 all-to-all-done
  20.9 0.6 shard_map.57
  21.4 18.4 %all_to_all.20.maps_ref = bf16[8,208,128]{2,1,0:T(8,128)(2,1)S(1)} all-to-all(bf16[8,208,128]{2,1,0:T(8,128)(2,1)S(1)} %shard_map.57), channel_id=1, replica_groups=mesh['z'=8,'y'=8,'head'=8] {'y'}, dimensions={0} | all-to-all | bytes 851968 | tf_op jit(solution)/shard_map/all_to_all | solution.py:457
  39.8 1.8 %shard_map.58 = (bf16[8,208,128]{2,1,0:T(8,128)(2,1)}, f32[3,192,128]{2,1,0:T(8,128)S(1)}) custom-call(bf16[8,208,128]{2,1,0:T(8,128)(2,1)S(1)} %all_to_all.20.maps_ref), custom_call_target="tpu_custom_call" | custom-call | tf_op jit(solution)/shard_map/pallas_call | solution.py:397
  41.6 0.0 copy-start.3
  41.7 0.7 copy-done.3
  42.4 10.1 %all-to-all-start.2 = ((bf16[8,208,128]{2,1,0:T(8,128)(2,1)}), bf16[8,208,128]{2,1,0:T(8,128)(2,1)S(1)}, u32[]{:S(2)}, u32[]{:S(2)}) async-start(bf16[8,208,128]{2,1,0:T(8,128)(2,1)} %get-tuple-element.24), calls=%async_computation.2 | async-start | bytes 851968 | tf_op jit(solution)/shard_map/all_to_all | solution.py:471
  52.4 0.0 copy-start.4
  52.4 5.3 %shard_map.59 = (bf16[4,512,256]{2,1,0:T(8,128)(2,1)S(1)}, f32[4,512,128]{2,1,0:T(8,128)S(1)}) custom-call(f32[4,512,128]{2,1,0:T(8,128)} %get-tuple-element.25.carry_ref, f32[4,512,128]{2,1,0:T(8,128)} %get-tuple-element.26.reply_ref, f32[4,512,128]{2,1,0:T(8,128)} %get-tuple-element.27.step_ref, f32[4,512,128]{2,1,0:T(8,128)} %get-tuple-element.28.source_ref, ...), custom_call_target="tpu_custom_call" | custom-call | tf_op jit(solution)/shard_map/pallas_call | solution.py:428
  57.7 0.0 copy-done.4
  57.8 0.5 shard_map.60
  58.3 0.0 copy-start.5
  58.3 0.7 copy-done.5
  59.0 7.8 %all-to-all-done.2.totals_ref = bf16[8,208,128]{2,1,0:T(8,128)(2,1)S(1)} async-done(((bf16[8,208,128]{2,1,0:T(8,128)(2,1)}), bf16[8,208,128]{2,1,0:T(8,128)(2,1)S(1)}, u32[]{:S(2)}, u32[]{:S(2)}) %all-to-all-start.2) | async-done | bytes 426016 | tf_op jit(solution)/shard_map/all_to_all | solution.py:471
  66.8 0.0 copy-start.6
  66.8 0.9 %copy-done.6 = f32[7,64,128]{2,1,0:T(8,128)S(1)} copy-done((f32[7,64,128]{2,1,0:T(8,128)S(1)}, f32[7,64,128]{2,1,0:T(8,128)}, u32[]{:S(2)}) %copy-start.6) | copy-done | bytes 229400
  67.7 1.3 %shard_map.61 = bf16[8,80,128]{2,1,0:T(8,128)(2,1)S(1)} custom-call(s32[1]{0:T(128)} %bitcast.1.place_ref, bf16[8,208,128]{2,1,0:T(8,128)(2,1)S(1)} %all-to-all-done.2.totals_ref, bf16[7,256,128]{2,1,0:T(8,128)(2,1)S(1)} %get-tuple-element.35.trans_ref, f32[7,64,128]{2,1,0:T(8,128)S(1)} %copy-done.6), custom_call_target="tpu_custom_call" | custom-call | tf_op jit(solution)/shard_map/pallas_call | solution.py:397
  69.0 11.8 %all_to_all.21.state_ref = bf16[8,80,128]{2,1,0:T(8,128)(2,1)S(1)} all-to-all(bf16[8,80,128]{2,1,0:T(8,128)(2,1)S(1)} %shard_map.61), channel_id=1, replica_groups=mesh['z'=8,'y'=8,'head'=8] {'y'}, dimensions={0} | all-to-all | bytes 327680 | tf_op jit(solution)/shard_map/all_to_all | solution.py:481
  80.8 1.4 %shard_map.62 = bf16[512,512]{1,0:T(8,128)(2,1)} custom-call(bf16[4,512,256]{2,1,0:T(8,128)(2,1)S(1)} %get-tuple-element.31.gain_ref, f32[4,512,128]{2,1,0:T(8,128)S(1)} %get-tuple-element.32.own_ref, bf16[8,80,128]{2,1,0:T(8,128)(2,1)S(1)} %all_to_all.21.state_ref), custom_call_target="tpu_custom_call" | custom-call | tf_op jit(solution)/shard_map/pallas_call | solution.py:397
  (1 shorter events, 0.0 us)
Async XLA Ops:
  0.0 11.5 %copy-start = (f32[512,512]{1,0:T(8,128)S(1)}, f32[512,512]{1,0:T(8,128)}, u32[]{:S(2)}) copy-start(f32[512,512]{1,0:T(8,128)} %decay_ref.1) | copy-start | bytes 3145732
  2.0 9.5 %copy-start.7 = (f32[4,512]{1,0:T(4,128)S(1)}, f32[4,512]{1,0:T(4,128)}, u32[]{:S(2)}) copy-start(f32[4,512]{1,0:T(4,128)} %param.8) | copy-start | bytes 24580
  2.0 9.5 %copy-start.1 = (bf16[512,512]{1,0:T(8,128)(2,1)S(1)}, bf16[512,512]{1,0:T(8,128)(2,1)}, u32[]{:S(2)}) copy-start(bf16[512,512]{1,0:T(8,128)(2,1)} %queries_ref.1) | copy-start | bytes 1572868
  2.0 18.8 %all-to-all-start = ((bf16[8,64,512]{2,1,0:T(8,128)(2,1)}), bf16[8,64,512]{2,1,0:T(8,128)(2,1)S(1)}, u32[]{:S(2)}, u32[]{:S(2)}) async-start(bf16[8,64,512]{2,1,0:T(8,128)(2,1)} %shard_map.56), calls=%async_computation | async-start | bytes 1048576 | tf_op jit(solution)/shard_map/all_to_all | solution.py:418
  11.5 1.0 %copy-start.2 = (bf16[512,512]{1,0:T(8,128)(2,1)S(1)}, bf16[512,512]{1,0:T(8,128)(2,1)}, u32[]{:S(2)}) copy-start(bf16[512,512]{1,0:T(8,128)(2,1)} %keys_ref.1) | copy-start | bytes 1572868
  41.6 0.7 copy-start.3
  42.4 24.4 %all-to-all-start.2 = ((bf16[8,208,128]{2,1,0:T(8,128)(2,1)}), bf16[8,208,128]{2,1,0:T(8,128)(2,1)S(1)}, u32[]{:S(2)}, u32[]{:S(2)}) async-start(bf16[8,208,128]{2,1,0:T(8,128)(2,1)} %get-tuple-element.24), calls=%async_computation.2 | async-start | bytes 851968 | tf_op jit(solution)/shard_map/all_to_all | solution.py:471
  52.4 5.3 %copy-start.4 = (f32[3,192,128]{2,1,0:T(8,128)S(1)}, f32[3,192,128]{2,1,0:T(8,128)}, u32[]{:S(2)}) copy-start(f32[3,192,128]{2,1,0:T(8,128)} %copy-done.3) | copy-start | bytes 884740
  58.3 0.7 copy-start.5
  66.8 0.9 %copy-start.6 = (f32[7,64,128]{2,1,0:T(8,128)S(1)}, f32[7,64,128]{2,1,0:T(8,128)}, u32[]{:S(2)}) copy-start(f32[7,64,128]{2,1,0:T(8,128)} %copy-done.5) | copy-start | bytes 688132
